TPU v7x, 256 devices: a whole 4x4x8 slice. The times are simulated.
256 devices in a mesh: row: 4 (over z_lo, core), col: 16 (over x, y), chan: 4 (over z_hi).
Axes of the slice: x: 4, y: 4, z: 8 (z_hi: 4, z_lo: 2; z = z_hi * 2 + z_lo), core: 2. Of those that a mesh axis runs over, the one named last changes fastest.
Arguments:
- pair: bfloat16 [1024, 1024, 128], P('row', 'col'), may hold values from -6 to 6
- pair_mask: int32 [1024, 1024], P('row', 'col'), may hold values 0 or 1
- ln_gain: float32 [128], replicated, may hold values from 0.1 to 1.9
- ln_bias: float32 [128], replicated, may hold values from -3 to 3
- left_value: bfloat16 [128, 128], P(None, 'chan'), may hold values from -0.5 to 0.5
- left_gate: bfloat16 [128, 128], P(None, 'chan'), may hold values from -0.5 to 0.5
- right_value: bfloat16 [128, 128], P(None, 'chan'), may hold values from -0.5 to 0.5
- right_gate: bfloat16 [128, 128], P(None, 'chan'), may hold values from -0.5 to 0.5
- hid_gain: float32 [128], replicated, may hold values from 0.1 to 1.9
- hid_bias: float32 [128], replicated, may hold values from -3 to 3
- out_weight: bfloat16 [128, 128], replicated, may hold values from -0.5 to 0.5
- out_gate: bfloat16 [128, 128], replicated, may hold values from -0.5 to 0.5
Outputs:
- update: bfloat16 [1024, 1024, 128], P('row', ('col', 'chan'))
All inputs are finite; a program needn't handle non-finite values. No bound on the sum of `pair_mask` on one device may be relied on, other than what follows from the above.
Results may differ from a plain program's by a relative error of at most 0.025.
Values may be sent and summed in bfloat16 or wider, within the bound.
No kernel may reach another device: no remote copies, remote signals or barrier semaphores. Data moves between devices by JAX's collectives and lax.ppermute only.
A program may use at most 128 MiB of HBM per device.

v0:
```python
import jax
import jax.numpy as jnp
from jax import lax
from jax.sharding import PartitionSpec as P


def on_device(
    pair,
    pair_mask,
    ln_gain,
    ln_bias,
    left_value,
    left_gate,
    right_value,
    right_gate,
    hid_gain,
    hid_bias,
    out_weight,
    out_gate,
):
    tile_cols = pair.shape[1]
    group_width = left_value.shape[1]
    out_cols = tile_cols // lax.axis_size("chan")
    group_index = lax.axis_index("chan")
    source = pair.astype(jnp.float32)
    centre = jnp.mean(source, axis=-1, keepdims=True)
    shifted = source - centre
    spread = jnp.mean(shifted * shifted, axis=-1, keepdims=True)
    normed = (shifted * lax.rsqrt(spread + 1e-05) * ln_gain + ln_bias).astype(jnp.bfloat16)
    weights = jnp.concatenate([left_value, left_gate, right_value, right_gate], axis=1)
    projected_all = jnp.einsum("ikc,cq->qik", normed, weights, preferred_element_type=jnp.float32)
    valid = pair_mask.astype(jnp.float32)[None, :, :]
    left = (
        jax.nn.sigmoid(projected_all[group_width : 2 * group_width])
        * projected_all[:group_width]
        * valid
    ).astype(jnp.bfloat16)
    right = (
        jax.nn.sigmoid(projected_all[3 * group_width :])
        * projected_all[2 * group_width : 3 * group_width]
        * valid
    ).astype(jnp.bfloat16)
    own_normed = lax.dynamic_slice_in_dim(normed, group_index * out_cols, out_cols, 1)
    gating = jax.nn.sigmoid(
        jnp.einsum("ijc,cd->ijd", own_normed, out_gate, preferred_element_type=jnp.float32)
    )
    right_all = lax.all_gather(right, "row", axis=1, tiled=True)
    product = lax.psum_scatter(
        jnp.einsum("hik,hjk->jhi", left, right_all, preferred_element_type=jnp.float32).astype(
            jnp.bfloat16
        ),
        "col",
        scatter_dimension=0,
        tiled=True,
    ).astype(jnp.float32)
    product = product.astype(jnp.bfloat16)
    widened = product.astype(jnp.float32)
    first_sums = jnp.sum(widened, axis=1)
    second_sums = jnp.sum(widened * widened, axis=1)
    first_sums, second_sums = (
        lax.psum(first_sums.astype(jnp.bfloat16), "chan").astype(jnp.float32),
        lax.psum(second_sums.astype(jnp.bfloat16), "chan").astype(jnp.float32),
    )
    total_width = group_width * lax.axis_size("chan")
    mean_hid = first_sums / total_width
    spread_hid = second_sums / total_width - mean_hid * mean_hid
    gain_part = lax.dynamic_slice_in_dim(hid_gain, group_index * group_width, group_width, 0)
    bias_part = lax.dynamic_slice_in_dim(hid_bias, group_index * group_width, group_width, 0)
    weight_rows = lax.dynamic_slice_in_dim(out_weight, group_index * group_width, group_width, 0)
    hidden = (
        (widened - mean_hid[:, None, :])
        * lax.rsqrt(spread_hid + 1e-05)[:, None, :]
        * gain_part[None, :, None]
        + bias_part[None, :, None]
    ).astype(jnp.bfloat16)
    mixed = lax.psum_scatter(
        jnp.einsum("jhi,hd->jid", hidden, weight_rows, preferred_element_type=jnp.float32).astype(
            jnp.bfloat16
        ),
        "chan",
        scatter_dimension=0,
        tiled=True,
    ).astype(jnp.float32)
    return (gating * jnp.transpose(mixed, (1, 0, 2))).astype(jnp.bfloat16)


def solution(mesh):
    return jax.shard_map(
        on_device,
        mesh=mesh,
        in_specs=(
            P("row", "col", None),
            P("row", "col"),
            P(),
            P(),
            P(None, "chan"),
            P(None, "chan"),
            P(None, "chan"),
            P(None, "chan"),
            P(),
            P(),
            P(),
            P(),
        ),
        out_specs=P("row", ("col", "chan"), None),
        check_vma=False,
    )
```

profile of v0, /device:TPU:1, one launch (start us, length us, event | category | flops | bytes accessed | tf_op | source)
XLA Modules:
  0.0 375.0 jit_solution(5184248092818221821)
XLA Ops:
  6.5 0.0 copy-start
  6.5 0.0 copy-start.3
  6.5 0.0 copy-start.9
  6.5 0.0 copy-start.8
  6.5 0.0 all-gather.2.cloned.1.call-start
  6.6 0.0 copy-start.1
  6.6 10.7 %convert_reduce_fusion = f32[256,64]{0,1:T(8,128)S(1)} fusion(bf16[256,64,128]{2,1,0:T(8,128)(2,1)} %param.12), kind=kLoop, calls=%fused_computation.2 | loop fusion | flops 4177920 | bytes 4259840 | tf_op jit(solution)/shard_map/reduce_sum | solution.py:26
  17.3 0.0 copy-done.1
  17.3 11.6 %fusion.2 = f32[256,64]{0,1:T(8,128)S(1)} fusion(f32[256,64]{0,1:T(8,128)S(1)} %broadcast_multiply_fusion, bf16[256,64,128]{2,1,0:T(8,128)(2,1)S(1)} %copy-done.1), kind=kLoop, calls=%fused_computation.5 | loop fusion | flops 8372224 | bytes 4325376 | tf_op jit(solution)/shard_map/reduce_sum | solution.py:28
  29.0 0.0 copy-done.3
  29.0 0.0 copy-done.9
  29.0 0.0 copy-done.8
  29.0 0.0 copy-start.4
  29.0 0.0 copy-start.5
  29.0 0.0 copy-start.6
  29.1 0.0 copy-start.7
  29.1 9.3 %fusion.5 = bf16[256,64,128]{2,0,1:T(8,128)(2,1)S(1)} fusion(f32[128]{0:T(128)S(1)} %copy-done.8, f32[128]{0:T(128)S(1)} %copy-done.9, f32[256,64]{0,1:T(8,128)S(1)} %add_rsqrt_fusion.1, f32[256,64]{0,1:T(8,128)S(1)} %broadcast_multiply_fusion, bf16[256,64,128]{2,1,0:T(8,128)(2,1)S(1)} %copy-done.1), kind=kLoop, calls=%fused_computation.8 | loop fusion | flops 12582912 | bytes 8520704 | tf_op jit(solution)/shard_map/convert_element_type | solution.py:29
  38.4 0.0 copy-done.4
  38.4 0.0 copy-done.5
  38.4 0.0 copy-done.6
  38.4 0.0 copy-done.7
  38.4 0.0 copy-start.2
  38.4 1.3 fusion.26
  39.7 0.7 copy-done.2
  40.3 2.4 fusion.13
  42.7 0.0 all-gather.2.cloned.1.call-update
  42.8 0.0 reduce-scatter.3.cloned.1.call-start
  42.8 53.4 %all-gather.2.cloned.1.call-done = bf16[32,1024,64]{1,0,2:T(8,128)(2,1)} async-done(((bf16[32,256,64]{1,0,2:T(8,128)(2,1)}), bf16[32,1024,64]{1,0,2:T(8,128)(2,1)}) %all-gather.2.cloned.1.call-update) | async-done | bytes 4194320 | tf_op jit(solution)/shard_map/all_gather | solution.py:47
  96.2 10.3 %convert_bitcast_fusion = bf16[1024,32,256]{2,0,1:T(8,128)(2,1)} fusion(bf16[32,1024,64]{1,0,2:T(8,128)(2,1)} %all-gather.2.cloned.1.call-done, bf16[32,256,64]{1,0,2:T(8,128)(2,1)S(1)} %get-tuple-element.7), kind=kOutput, calls=%fused_computation | convolution fusion | flops 1082130432 | bytes 22020096 | tf_op jit(solution)/shard_map/hik,hjk->jhi/dot_general | solution.py:49
  106.5 0.0 copy-start.11
  106.5 0.0 copy-start.12
  106.5 0.0 reduce-scatter.3.cloned.1.call-update
  106.5 0.0 all-reduce.3.cloned.1.call-start
  106.6 115.2 %reduce-scatter.3.cloned.1.call-done = bf16[64,32,256]{2,0,1:T(8,128)(2,1)} async-done(((bf16[1024,32,256]{2,0,1:T(8,128)(2,1)}), bf16[64,32,256]{2,0,1:T(8,128)(2,1)}) %reduce-scatter.3.cloned.1.call-update) | async-done | bytes 1048592 | tf_op jit(solution)/shard_map/reduce_scatter | solution.py:48
  221.8 2.1 fusion.11
  223.8 2.0 reduce_sum.41
  225.8 0.0 all-reduce.3.cloned.1.call-update
  225.8 0.3 reduce-scatter.5.cloned.1.call-start
  226.1 0.0 copy-done.11
  226.1 0.1 dynamic_slice.13
  226.2 0.0 copy-done.12
  226.2 0.1 dynamic_slice.14
  226.3 47.2 %all-reduce.3.cloned.1.call-done = (bf16[64,256]{1,0:T(8,128)(2,1)}, bf16[64,256]{1,0:T(8,128)(2,1)}) async-done(((bf16[64,256]{1,0:T(8,128)(2,1)}, bf16[64,256]{1,0:T(8,128)(2,1)}), (bf16[64,256]{1,0:T(8,128)(2,1)}, bf16[64,256]{1,0:T(8,128)(2,1)})) %all-reduce.3.cloned.1.call-update) | async-done | bytes 65552 | tf_op jit(solution)/shard_map/psum | solution.py:62
  273.5 0.8 convert_multiply_fusion.1
  274.3 1.6 fusion.10
  275.9 0.0 copy-done
  275.9 0.0 copy-start.10
  275.9 3.3 convolution_convert_fusion
  279.2 0.0 reduce-scatter.5.cloned.1.call-update
  279.2 85.3 %reduce-scatter.5.cloned.1.call-done = bf16[16,256,128]{2,1,0:T(8,128)(2,1)} async-done(((bf16[64,256,128]{2,1,0:T(8,128)(2,1)}), bf16[16,256,128]{2,1,0:T(8,128)(2,1)}) %reduce-scatter.5.cloned.1.call-update) | async-done | bytes 1048592 | tf_op jit(solution)/shard_map/reduce_scatter | solution.py:76
  364.5 0.0 copy-done.10
  364.5 2.2 fusion.22
  366.8 1.6 copy.17
  (3 shorter events, 0.0 us)
Async XLA Ops:
  6.5 269.4 %copy-start = (bf16[128,128]{1,0:T(8,128)(2,1)S(1)}, bf16[128,128]{1,0:T(8,128)(2,1)}, u32[]{:S(2)}) copy-start(bf16[128,128]{1,0:T(8,128)(2,1)} %param.22) | copy-start | bytes 98308
  6.5 22.4 %copy-start.3 = (s32[256,64]{0,1:T(8,128)S(1)}, s32[256,64]{0,1:T(8,128)}, u32[]{:S(2)}) copy-start(s32[256,64]{0,1:T(8,128)} %param.13) | copy-start | bytes 196612
  6.5 22.5 %copy-start.9 = (f32[128]{0:T(128)S(1)}, f32[128]{0:T(128)}, u32[]{:S(2)}) copy-start(f32[128]{0:T(128)} %param.14) | copy-start | bytes 1540
  6.5 22.5 %copy-start.8 = (f32[128]{0:T(128)S(1)}, f32[128]{0:T(128)}, u32[]{:S(2)}) copy-start(f32[128]{0:T(128)} %param.15) | copy-start | bytes 1540
  6.5 89.7 %all-gather.2.cloned.1.call-start = ((), (), s32[]{:S(2)}) async-start(), calls=%async_computation.2 | async-start | bytes 5242880 | tf_op jit(solution)/shard_map/all_gather | solution.py:47
  6.6 10.7 %copy-start.1 = (bf16[256,64,128]{2,1,0:T(8,128)(2,1)S(1)}, bf16[256,64,128]{2,1,0:T(8,128)(2,1)}, u32[]{:S(2)}) copy-start(bf16[256,64,128]{2,1,0:T(8,128)(2,1)} %param.12) | copy-start | bytes 12582916
  29.0 9.3 %copy-start.4 = (bf16[128,32]{0,1:T(8,128)(2,1)S(1)}, bf16[128,32]{0,1:T(8,128)(2,1)}, u32[]{:S(2)}) copy-start(bf16[128,32]{0,1:T(8,128)(2,1)} %param.19) | copy-start | bytes 24580
  29.0 9.3 %copy-start.5 = (bf16[128,32]{0,1:T(8,128)(2,1)S(1)}, bf16[128,32]{0,1:T(8,128)(2,1)}, u32[]{:S(2)}) copy-start(bf16[128,32]{0,1:T(8,128)(2,1)} %param.18) | copy-start | bytes 24580
  29.0 9.3 %copy-start.6 = (bf16[128,32]{0,1:T(8,128)(2,1)S(1)}, bf16[128,32]{0,1:T(8,128)(2,1)}, u32[]{:S(2)}) copy-start(bf16[128,32]{0,1:T(8,128)(2,1)} %param.17) | copy-start | bytes 24580
  29.1 9.3 %copy-start.7 = (bf16[128,32]{0,1:T(8,128)(2,1)S(1)}, bf16[128,32]{0,1:T(8,128)(2,1)}, u32[]{:S(2)}) copy-start(bf16[128,32]{0,1:T(8,128)(2,1)} %param.16) | copy-start | bytes 24580
  38.4 1.9 copy-start.2
  42.8 179.0 %reduce-scatter.3.cloned.1.call-start = ((), (), s32[]{:S(2)}) async-start(), calls=%async_computation.3 | async-start | bytes 17825792 | tf_op jit(solution)/shard_map/reduce_scatter | solution.py:48
  106.5 119.6 %copy-start.11 = (f32[128]{0:T(128)S(1)}, f32[128]{0:T(128)}, u32[]{:S(2)}) copy-start(f32[128]{0:T(128)} %param.20) | copy-start | bytes 1540
  106.5 119.7 %copy-start.12 = (f32[128]{0:T(128)S(1)}, f32[128]{0:T(128)}, u32[]{:S(2)}) copy-start(f32[128]{0:T(128)} %param.21) | copy-start | bytes 1540
  106.5 167.0 %all-reduce.3.cloned.1.call-start = ((), (), s32[]{:S(2)}) async-start(), calls=%async_computation.5 | async-start | bytes 131072 | tf_op jit(solution)/shard_map/psum | solution.py:62
  225.8 138.7 %reduce-scatter.5.cloned.1.call-start = ((), (), s32[]{:S(2)}) async-start(), calls=%async_computation.4 | async-start | bytes 5242880 | tf_op jit(solution)/shard_map/reduce_scatter | solution.py:76
  275.9 88.6 %copy-start.10 = (bf16[128,128]{1,0:T(8,128)(2,1)S(1)}, bf16[128,128]{1,0:T(8,128)(2,1)}, u32[]{:S(2)}) copy-start(bf16[128,128]{1,0:T(8,128)(2,1)} %param.23) | copy-start | bytes 98308
Sparse Core Ops, SparseCore 0:
  42.9 53.2 all-gather.1
  106.6 115.0 reduce-scatter.2
  226.0 47.4 all-reduce.2
  279.4 85.1 reduce-scatter.4
where the time goes:
time: 375 us
  waiting for transfers between devices  301 us (80%)
  other arithmetic  40.5 us (11%)
  matrix products  17 us (5%)
  between operations  13.3 us (4%)
    reduce_scatter x1, waiting for transfers between devices, on_device(): lax.psum_scatter(jnp.einsum('hik,hjk->jhi', left, right_all, preferred_el...  115 us
    reduce_scatter x1, waiting for transfers between devices, on_device(): lax.psum_scatter(jnp.einsum('jhi,hd->jid', hidden, weight_rows, preferred...  85.3 us
    all_gather x1, waiting for transfers between devices, on_device(): right_all = lax.all_gather(right, 'row', axis=1, tiled=True)  53.4 us
    psum x1, waiting for transfers between devices, on_device(): lax.psum(second_sums.astype(jnp.bfloat16), 'chan').astype(jnp.float32)  47.2 us
    reduce_sum x1, other arithmetic, on_device(): spread = jnp.mean(shifted * shifted, axis=-1, keepdims=True)  11.6 us
    reduce_sum x1, other arithmetic, on_device(): centre = jnp.mean(source, axis=-1, keepdims=True)  10.7 us
    dot_general x1, matrix products, on_device(): jnp.einsum('hik,hjk->jhi', left, right_all, preferred_element_type=jnp.fl...  10.3 us
    convert_element_type x1, other arithmetic, on_device(): (shifted * lax.rsqrt(spread + 1e-05) * ln_gain + ln_bias).astype(jnp.bflo...  9.28 us
  transfers between devices with their start and end apart: 4, of which 4 were waited for; matrix products, arithmetic and copies ran while one was open for 0% of the time, Pallas kernels for 0%

commit v1 on v0

--- a/solution.py
+++ b/solution.py
@@ -44,7 +44,15 @@
     gating = jax.nn.sigmoid(
         jnp.einsum("ijc,cd->ijd", own_normed, out_gate, preferred_element_type=jnp.float32)
     )
-    right_all = lax.all_gather(right, "row", axis=1, tiled=True)
+    right_all = jnp.concatenate(
+        lax.all_to_all(
+            jnp.stack([right for _ in range(lax.axis_size("row"))]),
+            axis_name="row",
+            split_axis=0,
+            concat_axis=0,
+        ),
+        1,
+    )
     product = lax.psum_scatter(
         jnp.einsum("hik,hjk->jhi", left, right_all, preferred_element_type=jnp.float32).astype(
             jnp.bfloat16

time: 375 us -> 375 us (level)
  blocking collectives: 0 us -> 52.9 us
  waiting for transfers between devices: 301 us -> 249 us
    all_gather x1 -> x0, waiting for transfers between devices: 53.4 us -> none  [on_device(): right_all = lax.all_gather(right, 'row', axis=1, tiled=True)]
    all_to_all x0 -> x1, blocking collectives: none -> 52.9 us  [on_device(): lax.all_to_all(jnp.stack([right for _ in range(lax.axis_size('row'))]), a...]
  transfers between devices with their start and end apart: 4 -> 3, of which waited for: 4 -> 3; matrix products, arithmetic and copies ran while one was open for 0% -> 0% of each run, Pallas kernels for 0% -> 0%
where the time goes in v1:
time: 375 us
  waiting for transfers between devices  249 us (66%)
  blocking collectives  52.9 us (14%)
  other arithmetic  39.6 us (11%)
  matrix products  14.9 us (4%)
  between operations  13.4 us (4%)
  local copies, waits for them, and re-layouts  4.14 us (1%)
    reduce_scatter x1, waiting for transfers between devices, on_device(): lax.psum_scatter(jnp.einsum('hik,hjk->jhi', left, right_all, preferred_el...  117 us
    reduce_scatter x1, waiting for transfers between devices, on_device(): lax.psum_scatter(jnp.einsum('jhi,hd->jid', hidden, weight_rows, preferred...  85.3 us
    all_to_all x1, blocking collectives, on_device(): lax.all_to_all(jnp.stack([right for _ in range(lax.axis_size('row'))]), a...  52.9 us
    psum x1, waiting for transfers between devices, on_device(): lax.psum(second_sums.astype(jnp.bfloat16), 'chan').astype(jnp.float32)  47.1 us
    reduce_sum x1, other arithmetic, on_device(): spread = jnp.mean(shifted * shifted, axis=-1, keepdims=True)  11.6 us
    reduce_sum x1, other arithmetic, on_device(): centre = jnp.mean(source, axis=-1, keepdims=True)  10.7 us
    convert_element_type x1, other arithmetic, on_device(): (shifted * lax.rsqrt(spread + 1e-05) * ln_gain + ln_bias).astype(jnp.bflo...  9.28 us
    dot_general x1, matrix products, on_device(): jnp.einsum('hik,hjk->jhi', left, right_all, preferred_element_type=jnp.fl...  8.16 us
  transfers between devices with their start and end apart: 3, of which 3 were waited for; matrix products, arithmetic and copies ran while one was open for 0% of the time, Pallas kernels for 0%

profile of v1, /device:TPU:1, one launch (start us, length us, event | category | flops | bytes accessed | tf_op | source)
XLA Modules:
  0.0 374.7 jit_solution(11524459674680655166)
XLA Ops:
  6.5 0.0 copy-start
  6.5 0.0 copy-start.3
  6.5 0.0 copy-start.9
  6.5 0.0 copy-start.8
  6.5 0.0 reduce-scatter.3.cloned.1.call-start
  6.6 0.0 copy-start.1
  6.6 10.7 %convert_reduce_fusion = f32[256,64]{0,1:T(8,128)S(1)} fusion(bf16[256,64,128]{2,1,0:T(8,128)(2,1)} %param.12), kind=kLoop, calls=%fused_computation.2 | loop fusion | flops 4177920 | bytes 4259840 | tf_op jit(solution)/shard_map/reduce_sum | solution.py:26
  17.3 0.0 copy-done.1
  17.3 11.6 %fusion.2 = f32[256,64]{0,1:T(8,128)S(1)} fusion(f32[256,64]{0,1:T(8,128)S(1)} %broadcast_multiply_fusion, bf16[256,64,128]{2,1,0:T(8,128)(2,1)S(1)} %copy-done.1), kind=kLoop, calls=%fused_computation.5 | loop fusion | flops 8372224 | bytes 4325376 | tf_op jit(solution)/shard_map/reduce_sum | solution.py:28
  29.0 0.0 copy-done.3
  29.0 0.0 copy-done.9
  29.0 0.0 copy-done.8
  29.0 0.0 copy-start.4
  29.0 0.0 copy-start.5
  29.0 0.0 copy-start.6
  29.1 0.0 copy-start.7
  29.1 9.3 %fusion.5 = bf16[256,64,128]{2,0,1:T(8,128)(2,1)S(1)} fusion(f32[128]{0:T(128)S(1)} %copy-done.8, f32[128]{0:T(128)S(1)} %copy-done.9, f32[256,64]{0,1:T(8,128)S(1)} %add_rsqrt_fusion.1, f32[256,64]{0,1:T(8,128)S(1)} %broadcast_multiply_fusion, bf16[256,64,128]{2,1,0:T(8,128)(2,1)S(1)} %copy-done.1), kind=kLoop, calls=%fused_computation.8 | loop fusion | flops 12582912 | bytes 8520704 | tf_op jit(solution)/shard_map/convert_element_type | solution.py:29
  38.4 0.0 copy-done.4
  38.4 0.0 copy-done.5
  38.4 0.0 copy-done.6
  38.4 0.0 copy-done.7
  38.4 0.0 copy-start.2
  38.4 1.3 fusion.25
  39.7 0.7 copy-done.2
  40.3 1.4 fusion.12
  41.8 0.6 copy.19
  42.4 0.5 stack.2
  42.9 52.9 %all_to_all.5 = bf16[4,32,256,64]{2,3,1,0:T(8,128)(2,1)S(1)} all-to-all(bf16[4,32,256,64]{2,3,1,0:T(8,128)(2,1)S(1)} %stack.2), channel_id=1, replica_groups=mesh['row'=4,'col'=16,'chan'=4] {'row'}, dimensions={0} | all-to-all | bytes 8388608 | tf_op jit(solution)/shard_map/all_to_all | solution.py:48
  95.8 0.5 copy.24
  96.3 8.2 %convert_bitcast_fusion = bf16[1024,32,256]{2,0,1:T(8,128)(2,1)} fusion(bf16[32,1024,64]{1,2,0:T(8,128)(2,1)S(1)} %bitcast.20, bf16[32,256,64]{1,0,2:T(8,128)(2,1)S(1)} %get-tuple-element.7), kind=kOutput, calls=%fused_computation | convolution fusion | flops 1082130432 | bytes 22020096 | tf_op jit(solution)/shard_map/hik,hjk->jhi/dot_general | solution.py:57
  104.5 0.0 copy-start.11
  104.5 0.0 copy-start.12
  104.5 0.0 reduce-scatter.3.cloned.1.call-update
  104.5 0.0 all-reduce.3.cloned.1.call-start
  104.6 117.0 %reduce-scatter.3.cloned.1.call-done = bf16[64,32,256]{2,0,1:T(8,128)(2,1)} async-done(((bf16[1024,32,256]{2,0,1:T(8,128)(2,1)}), bf16[64,32,256]{2,0,1:T(8,128)(2,1)}) %reduce-scatter.3.cloned.1.call-update) | async-done | bytes 1048592 | tf_op jit(solution)/shard_map/reduce_scatter | solution.py:56
  221.6 2.1 fusion.10
  223.7 2.0 reduce_sum.41
  225.7 0.0 all-reduce.3.cloned.1.call-update
  225.7 0.3 reduce-scatter.5.cloned.1.call-start
  226.0 0.0 copy-done.11
  226.0 0.1 dynamic_slice.13
  226.0 0.0 copy-done.12
  226.0 0.1 dynamic_slice.14
  226.1 47.1 %all-reduce.3.cloned.1.call-done = (bf16[64,256]{1,0:T(8,128)(2,1)}, bf16[64,256]{1,0:T(8,128)(2,1)}) async-done(((bf16[64,256]{1,0:T(8,128)(2,1)}, bf16[64,256]{1,0:T(8,128)(2,1)}), (bf16[64,256]{1,0:T(8,128)(2,1)}, bf16[64,256]{1,0:T(8,128)(2,1)})) %all-reduce.3.cloned.1.call-update) | async-done | bytes 65552 | tf_op jit(solution)/shard_map/psum | solution.py:70
  273.2 0.8 convert_multiply_fusion.1
  274.0 1.6 fusion.9
  275.7 0.0 copy-done
  275.7 0.0 copy-start.10
  275.7 3.3 convolution_convert_fusion
  279.0 0.0 reduce-scatter.5.cloned.1.call-update
  279.0 85.3 %reduce-scatter.5.cloned.1.call-done = bf16[16,256,128]{2,1,0:T(8,128)(2,1)} async-done(((bf16[64,256,128]{2,1,0:T(8,128)(2,1)}), bf16[16,256,128]{2,1,0:T(8,128)(2,1)}) %reduce-scatter.5.cloned.1.call-update) | async-done | bytes 1048592 | tf_op jit(solution)/shard_map/reduce_scatter | solution.py:84
  364.3 0.0 copy-done.10
  364.3 2.2 fusion.21
  366.5 1.6 copy.23
  (3 shorter events, 0.0 us)
Async XLA Ops:
  6.5 269.1 %copy-start = (bf16[128,128]{1,0:T(8,128)(2,1)S(1)}, bf16[128,128]{1,0:T(8,128)(2,1)}, u32[]{:S(2)}) copy-start(bf16[128,128]{1,0:T(8,128)(2,1)} %param.22) | copy-start | bytes 98308
  6.5 22.4 %copy-start.3 = (s32[256,64]{0,1:T(8,128)S(1)}, s32[256,64]{0,1:T(8,128)}, u32[]{:S(2)}) copy-start(s32[256,64]{0,1:T(8,128)} %param.13) | copy-start | bytes 196612
  6.5 22.5 %copy-start.9 = (f32[128]{0:T(128)S(1)}, f32[128]{0:T(128)}, u32[]{:S(2)}) copy-start(f32[128]{0:T(128)} %param.14) | copy-start | bytes 1540
  6.5 22.5 %copy-start.8 = (f32[128]{0:T(128)S(1)}, f32[128]{0:T(128)}, u32[]{:S(2)}) copy-start(f32[128]{0:T(128)} %param.15) | copy-start | bytes 1540
  6.5 215.1 %reduce-scatter.3.cloned.1.call-start = ((), (), s32[]{:S(2)}) async-start(), calls=%async_computation.3 | async-start | bytes 17825792 | tf_op jit(solution)/shard_map/reduce_scatter | solution.py:56
  6.6 10.7 %copy-start.1 = (bf16[256,64,128]{2,1,0:T(8,128)(2,1)S(1)}, bf16[256,64,128]{2,1,0:T(8,128)(2,1)}, u32[]{:S(2)}) copy-start(bf16[256,64,128]{2,1,0:T(8,128)(2,1)} %param.12) | copy-start | bytes 12582916
  29.0 9.3 %copy-start.4 = (bf16[128,32]{0,1:T(8,128)(2,1)S(1)}, bf16[128,32]{0,1:T(8,128)(2,1)}, u32[]{:S(2)}) copy-start(bf16[128,32]{0,1:T(8,128)(2,1)} %param.19) | copy-start | bytes 24580
  29.0 9.3 %copy-start.5 = (bf16[128,32]{0,1:T(8,128)(2,1)S(1)}, bf16[128,32]{0,1:T(8,128)(2,1)}, u32[]{:S(2)}) copy-start(bf16[128,32]{0,1:T(8,128)(2,1)} %param.18) | copy-start | bytes 24580
  29.0 9.3 %copy-start.6 = (bf16[128,32]{0,1:T(8,128)(2,1)S(1)}, bf16[128,32]{0,1:T(8,128)(2,1)}, u32[]{:S(2)}) copy-start(bf16[128,32]{0,1:T(8,128)(2,1)} %param.17) | copy-start | bytes 24580
  29.1 9.3 %copy-start.7 = (bf16[128,32]{0,1:T(8,128)(2,1)S(1)}, bf16[128,32]{0,1:T(8,128)(2,1)}, u32[]{:S(2)}) copy-start(bf16[128,32]{0,1:T(8,128)(2,1)} %param.16) | copy-start | bytes 24580
  38.4 1.9 copy-start.2
  104.5 121.5 %copy-start.11 = (f32[128]{0:T(128)S(1)}, f32[128]{0:T(128)}, u32[]{:S(2)}) copy-start(f32[128]{0:T(128)} %param.20) | copy-start | bytes 1540
  104.5 121.5 %copy-start.12 = (f32[128]{0:T(128)S(1)}, f32[128]{0:T(128)}, u32[]{:S(2)}) copy-start(f32[128]{0:T(128)} %param.21) | copy-start | bytes 1540
  104.5 168.7 %all-reduce.3.cloned.1.call-start = ((), (), s32[]{:S(2)}) async-start(), calls=%async_computation.5 | async-start | bytes 131072 | tf_op jit(solution)/shard_map/psum | solution.py:70
  225.7 138.6 %reduce-scatter.5.cloned.1.call-start = ((), (), s32[]{:S(2)}) async-start(), calls=%async_computation.4 | async-start | bytes 5242880 | tf_op jit(solution)/shard_map/reduce_scatter | solution.py:84
  275.7 88.6 %copy-start.10 = (bf16[128,128]{1,0:T(8,128)(2,1)S(1)}, bf16[128,128]{1,0:T(8,128)(2,1)}, u32[]{:S(2)}) copy-start(bf16[128,128]{1,0:T(8,128)(2,1)} %param.23) | copy-start | bytes 98308
Sparse Core Ops, SparseCore 0:
  104.7 116.8 reduce-scatter.2
  225.8 47.3 all-reduce.2
  279.1 85.1 reduce-scatter.4
